TPU v7x, 32 devices: a whole 2x2x4 slice. The times are simulated.
32 devices in a mesh: dp: 4 (over z), table: 8 (over y, x, core).
Axes of the slice: x: 2, y: 2, z: 4, core: 2. Of those that a mesh axis runs over, the one named last changes fastest.
Arguments:
- dense_feats: bfloat16 [4096, 13], P(('dp', 'table')), may hold values from -6 to 6
- lookup_ids: int32 [32, 8, 4096], P('table', None, 'dp'), may hold values from 0 to 2047
- lookup_counts: int32 [32, 4096], P('table', 'dp'), may hold values from 0 to 8
- shard_table: int32 [32], replicated, may hold values from 0 to 25, as said below
- embed_tables: bfloat16 [32, 2048, 128], P('table'), may hold values from -6 to 6
- first_layer: bfloat16 [13, 512], replicated, may hold values from -1.75 to 1.75
- first_offset: float32 [512], replicated, may hold values from -3 to 3
- second_layer: bfloat16 [512, 256], replicated, may hold values from -0.25 to 0.25
- second_offset: float32 [256], replicated, may hold values from -3 to 3
- third_layer: bfloat16 [256, 128], replicated, may hold values from -0.375 to 0.375
- third_offset: float32 [128], replicated, may hold values from -3 to 3
- cross_down: bfloat16 [3456, 512], P(None, 'table'), may hold values from -0.109375 to 0.109375
- cross_up: bfloat16 [512, 3456], P('table'), may hold values from -0.25 to 0.25
- cross_bias: float32 [3456], replicated, may hold values from -3 to 3
- cotangent: bfloat16 [4096, 3456], P(('dp', 'table')), may hold values from -0.059814453 to 0.059814453
Outputs:
- table_grad: float32 [32, 2048, 128], P('table', 'dp')
- first_layer_grad: float32 [13, 512], replicated
- first_offset_grad: float32 [512], replicated
- second_layer_grad: float32 [512, 256], replicated
- second_offset_grad: float32 [256], replicated
- third_layer_grad: float32 [256, 128], replicated
- third_offset_grad: float32 [128], replicated
- cross_bias_grad: float32 [3456], replicated
Inputs may be any that keep to these rules, and one draw needn't show every extreme that they name: `shard_table`: every table has at least one shard.
All inputs are finite; a program needn't handle non-finite values.
Results may differ from a plain program's by a relative error of at most 0.0085.
Values may be sent and summed in bfloat16 or wider, within the bound.
A program may use at most 64 MiB of HBM per device.

v0:
```python
import math

import jax
import jax.numpy as jnp
from jax import lax
from jax.sharding import PartitionSpec as P

TABLES = 26


def silu_slope(value):
    sigmoid = 1.0 / (1.0 + jnp.exp(-value))
    return sigmoid * (1.0 + value * (1.0 - sigmoid))


def hit_counts(index_block, count_block, row_total):
    iota_rows = lax.broadcasted_iota(jnp.int32, (index_block.shape[1], row_total), 1)
    totals = jnp.zeros((index_block.shape[1], row_total), jnp.bfloat16)
    for slot_index in range(index_block.shape[0]):
        matched = (index_block[slot_index][:, None] == iota_rows) & (
            count_block[:, None] > slot_index
        )
        totals = totals + matched.astype(jnp.bfloat16)
    return totals


def split_blocks(shard_index, shard_count, block_size):
    hot_total, batch_total = shard_index.shape
    blocks = batch_total // block_size
    index_blocks = shard_index.reshape(hot_total, blocks, block_size).transpose(1, 0, 2)
    count_blocks = shard_count.reshape(blocks, block_size)
    return (index_blocks, count_blocks, blocks)


def pool_shard(table_rows, shard_index, shard_count, block_size):
    index_blocks, count_blocks, blocks = split_blocks(shard_index, shard_count, block_size)

    def pool_one_block(inputs):
        hit_table = hit_counts(inputs[0], inputs[1], table_rows.shape[0])
        return jnp.dot(hit_table, table_rows, preferred_element_type=jnp.float32)

    pooled = lax.map(pool_one_block, (index_blocks, count_blocks))
    return pooled.reshape(shard_index.shape[1], table_rows.shape[1])


def shard_gradient(shard_index, shard_count, grad_rows, row_total, block_size):
    index_blocks, count_blocks, blocks = split_blocks(shard_index, shard_count, block_size)
    grad_blocks = grad_rows.reshape(blocks, block_size, grad_rows.shape[1])

    def shard_one_block(running, inputs):
        hit_table = hit_counts(inputs[0], inputs[1], row_total)
        update = lax.dot_general(
            hit_table, inputs[2], (((0,), (0,)), ((), ())), preferred_element_type=jnp.float32
        )
        return (running + update, None)

    result, unused = lax.scan(
        shard_one_block,
        jnp.zeros((row_total, grad_rows.shape[1]), jnp.float32),
        (index_blocks, count_blocks, grad_blocks),
    )
    return result


def bottom_pass(
    dense_rows, first_layer, first_offset, second_layer, second_offset, third_layer, third_offset
):
    first_pre = jnp.dot(dense_rows, first_layer, preferred_element_type=jnp.float32) + first_offset
    first_act = jax.nn.silu(first_pre).astype(jnp.bfloat16)
    second_pre = (
        jnp.dot(first_act, second_layer, preferred_element_type=jnp.float32) + second_offset
    )
    second_act = jax.nn.silu(second_pre).astype(jnp.bfloat16)
    third_pre = jnp.dot(second_act, third_layer, preferred_element_type=jnp.float32) + third_offset
    bottom_out = jax.nn.silu(third_pre).astype(jnp.bfloat16)
    return (bottom_out, (first_pre, first_act, second_pre, second_act, third_pre))


def bottom_back(dense_rows, saved, second_layer, third_layer, bottom_grad):
    first_pre, first_act, second_pre, second_act, third_pre = saved
    contract = (((0,), (0,)), ((), ()))
    back_dims = (((1,), (1,)), ((), ()))
    third_delta = (silu_slope(third_pre) * bottom_grad.astype(jnp.float32)).astype(jnp.bfloat16)
    third_grad = lax.dot_general(
        second_act, third_delta, contract, preferred_element_type=jnp.float32
    )
    third_bias = jnp.sum(third_delta.astype(jnp.float32), axis=0)
    second_back = lax.dot_general(
        third_delta, third_layer, back_dims, preferred_element_type=jnp.float32
    )
    second_delta = (silu_slope(second_pre) * second_back).astype(jnp.bfloat16)
    second_grad = lax.dot_general(
        first_act, second_delta, contract, preferred_element_type=jnp.float32
    )
    second_bias = jnp.sum(second_delta.astype(jnp.float32), axis=0)
    first_back = lax.dot_general(
        second_delta, second_layer, back_dims, preferred_element_type=jnp.float32
    )
    first_delta = (silu_slope(first_pre) * first_back).astype(jnp.bfloat16)
    first_grad = lax.dot_general(
        dense_rows, first_delta, contract, preferred_element_type=jnp.float32
    )
    first_bias = jnp.sum(first_delta.astype(jnp.float32), axis=0)
    return (first_grad, first_bias, second_grad, second_bias, third_grad, third_bias)


def local(
    dense_feats,
    lookup_ids,
    lookup_counts,
    shard_table,
    embed_tables,
    first_layer,
    first_offset,
    second_layer,
    second_offset,
    third_layer,
    third_offset,
    cross_down,
    cross_up,
    cross_bias,
    cotangent,
):
    local_shards, row_total, width = embed_tables.shape
    batch_group = lookup_ids.shape[2]
    block_size = math.gcd(batch_group, 1024)
    examples = dense_feats.shape[0]
    back_dims = (((1,), (1,)), ((), ()))
    pooled = jnp.stack(
        [
            pool_shard(
                embed_tables[shard_pos], lookup_ids[shard_pos], lookup_counts[shard_pos], block_size
            )
            for shard_pos in range(local_shards)
        ],
        axis=1,
    ).astype(jnp.bfloat16)
    arrived = lax.all_to_all(pooled, "table", split_axis=0, concat_axis=1, tiled=True)
    table_onehot = (
        shard_table[:, None] == lax.broadcasted_iota(jnp.int32, (shard_table.shape[0], TABLES), 1)
    ).astype(jnp.bfloat16)
    table_pooled = jnp.einsum(
        "bse,st->bte", arrived, table_onehot, preferred_element_type=jnp.float32
    ).astype(jnp.bfloat16)
    bottom_out, saved = bottom_pass(
        dense_feats,
        first_layer,
        first_offset,
        second_layer,
        second_offset,
        third_layer,
        third_offset,
    )
    cross_input = jnp.concatenate([bottom_out[:, None, :], table_pooled], axis=1).reshape(
        examples, -1
    )
    down_whole = lax.all_gather(cross_down, "table", axis=1, tiled=True)
    up_whole = lax.all_gather(cross_up, "table", axis=0, tiled=True)
    low_rank = jnp.dot(cross_input, down_whole, preferred_element_type=jnp.float32).astype(
        jnp.bfloat16
    )
    mixing = jnp.dot(low_rank, up_whole, preferred_element_type=jnp.float32) + cross_bias
    cot_float = cotangent.astype(jnp.float32)
    mix_grad = cot_float * cross_input.astype(jnp.float32)
    bias_part = jnp.sum(mix_grad, axis=0)
    rank_grad = lax.dot_general(
        mix_grad.astype(jnp.bfloat16), up_whole, back_dims, preferred_element_type=jnp.float32
    ).astype(jnp.bfloat16)
    input_grad = (
        cot_float * (mixing + 1.0)
        + lax.dot_general(rank_grad, down_whole, back_dims, preferred_element_type=jnp.float32)
    ).astype(jnp.bfloat16)
    input_grad = input_grad.reshape(examples, TABLES + 1, width)
    bottom_grad = input_grad[:, 0, :]
    shard_grads = jnp.einsum(
        "bte,st->bse", input_grad[:, 1:, :], table_onehot, preferred_element_type=jnp.float32
    ).astype(jnp.bfloat16)
    returned = lax.all_to_all(shard_grads, "table", split_axis=1, concat_axis=0, tiled=True)
    local_grad = jnp.stack(
        [
            shard_gradient(
                lookup_ids[shard_pos],
                lookup_counts[shard_pos],
                returned[:, shard_pos, :],
                row_total,
                block_size,
            )
            for shard_pos in range(local_shards)
        ],
        axis=0,
    )
    table_grad = lax.psum_scatter(local_grad, "dp", scatter_dimension=1, tiled=True)
    partial_grads = bottom_back(dense_feats, saved, second_layer, third_layer, bottom_grad)
    summed = lax.psum(
        (
            partial_grads[0],
            partial_grads[1],
            partial_grads[2],
            partial_grads[3],
            partial_grads[4],
            partial_grads[5],
            bias_part,
        ),
        ("dp", "table"),
    )
    return (table_grad, summed[0], summed[1], summed[2], summed[3], summed[4], summed[5], summed[6])


def solution(mesh):
    placed = (
        P(("dp", "table"), None),
        P("table", None, "dp"),
        P("table", "dp"),
        P(),
        P("table", None, None),
        P(),
        P(),
        P(),
        P(),
        P(),
        P(),
        P(None, "table"),
        P("table", None),
        P(),
        P(("dp", "table"), None),
    )
    return jax.shard_map(
        local,
        mesh=mesh,
        in_specs=placed,
        out_specs=(P("table", "dp", None), P(), P(), P(), P(), P(), P(), P()),
        check_vma=False,
    )
```

profile of v0, /device:TPU:0, one launch (start us, length us, event | category | flops | bytes accessed | tf_op | source)
XLA Modules:
  0.0 352.9 jit_solution(10390287300241954063)
XLA Ops:
  7.2 0.7 all-gather.3.cloned.1.call-update
  8.0 0.7 all-gather.5.cloned.1.call-update
  8.7 1.4 fusion.125
  10.1 1.2 fusion.126
  11.3 1.3 compare_reduce_fusion.31
  12.5 14.5 %fusion.74 = bf16[1024,2048]{1,0:T(8,128)(2,1)S(1)} fusion(s32[1024]{0:T(1024)S(1)} %bitcast.150, s32[1024]{0:T(1024)S(1)} %bitcast.151, s32[1024]{0:T(1024)S(1)} %bitcast.152, s32[1024]{0:T(1024)S(1)} %bitcast.153, s32[1024]{0:T(1024)S(1)} %bitcast.154, s32[1024]{0:T(1024)S(1)} %bitcast.155, s32[1024]{0:T(1024)S(1)} %bitcast.156, s32[1024]{0:T(1024)S(1)} %bitcast.157, ...), kind=kLoop, calls=%fused_computation.108 | loop fusion | flops 83886080 | bytes 4235264 | tf_op jit(solution)/shard_map/while/body/eval_jaxpr/add | solution.py:23
  27.0 1.3 fusion.101
  28.3 14.5 %fusion.81 = bf16[1024,2048]{1,0:T(8,128)(2,1)S(1)} fusion(s32[1024]{0:T(1024)S(1)} %bitcast.146, s32[1024]{0:T(1024)S(1)} %bitcast.147, s32[1024]{0:T(1024)S(1)} %bitcast.148, s32[1024]{0:T(1024)S(1)} %bitcast.149, s32[1024]{0:T(1024)S(1)} %bitcast.167, s32[1024]{0:T(1024)S(1)} %bitcast.168, s32[1024]{0:T(1024)S(1)} %bitcast.169, s32[1024]{0:T(1024)S(1)} %bitcast.170, ...), kind=kLoop, calls=%fused_computation.115 | loop fusion | flops 83886080 | bytes 4235264 | tf_op jit(solution)/shard_map/while/body/eval_jaxpr/add | solution.py:23
  42.8 1.2 fusion.100
  44.1 14.5 %fusion.88 = bf16[1024,2048]{1,0:T(8,128)(2,1)S(1)} fusion(s32[1024]{0:T(1024)S(1)} %bitcast.161, s32[1024]{0:T(1024)S(1)} %bitcast.162, s32[1024]{0:T(1024)S(1)} %bitcast.163, s32[1024]{0:T(1024)S(1)} %bitcast.164, s32[1024]{0:T(1024)S(1)} %bitcast.165, s32[1024]{0:T(1024)S(1)} %bitcast.166, s32[1024]{0:T(1024)S(1)} %bitcast.160, s32[1024]{0:T(1024)S(1)} %bitcast.145, ...), kind=kLoop, calls=%fused_computation.122 | loop fusion | flops 83886080 | bytes 4235264 | tf_op jit(solution)/shard_map/while/body/eval_jaxpr/add | solution.py:23
  58.6 1.2 fusion.99
  59.8 14.5 %fusion.67 = bf16[1024,2048]{1,0:T(8,128)(2,1)S(1)} fusion(s32[1024]{0:T(1024)S(1)} %bitcast.158, s32[1024]{0:T(1024)S(1)} %bitcast.159, s32[1024]{0:T(1024)S(1)} %bitcast.139, s32[1024]{0:T(1024)S(1)} %bitcast.140, s32[1024]{0:T(1024)S(1)} %bitcast.141, s32[1024]{0:T(1024)S(1)} %bitcast.142, s32[1024]{0:T(1024)S(1)} %bitcast.143, s32[1024]{0:T(1024)S(1)} %bitcast.144, ...), kind=kLoop, calls=%fused_computation.101 | loop fusion | flops 83886080 | bytes 4235264 | tf_op jit(solution)/shard_map/while/body/eval_jaxpr/add | solution.py:23
  74.3 1.2 fusion.102
  75.8 0.5 copy-done.6
  76.3 1.8 copy.45
  78.1 5.2 %all-to-all-start = ((bf16[1024,4,128]{2,1,0:T(4,128)(2,1)}), bf16[1024,4,128]{2,1,0:T(4,128)(2,1)S(1)}, u32[]{:S(2)}, u32[]{:S(2)}) async-start(bf16[1024,4,128]{2,1,0:T(4,128)(2,1)} %copy.45), calls=%async_computation | async-start | bytes 2097152 | tf_op jit(solution)/shard_map/all_to_all | solution.py:138
  84.1 14.5 %all-to-all-done = bf16[1024,4,128]{2,1,0:T(4,128)(2,1)S(1)} async-done(((bf16[1024,4,128]{2,1,0:T(4,128)(2,1)}), bf16[1024,4,128]{2,1,0:T(4,128)(2,1)S(1)}, u32[]{:S(2)}, u32[]{:S(2)}) %all-to-all-start) | async-done | bytes 1048608 | tf_op jit(solution)/shard_map/all_to_all | solution.py:138
  98.6 0.4 copy.46
  99.0 0.6 fusion.97
  99.6 1.5 pad_maximum_fusion.2
  101.1 2.3 copy.49
  103.4 1.0 copy.50
  104.5 6.2 %fusion.65 = f32[128,3456]{1,0:T(8,128)} fusion(bf16[512,3456]{1,0:T(8,128)(2,1)} %all-gather.5.cloned.1.call-done, bf16[128,3456]{1,0:T(8,128)(2,1)S(1)} %copy-done.8, bf16[128,3456]{0,1:T(8,128)(2,1)S(1)} %bitcast.129, bf16[3456,512]{0,1:T(8,128)(2,1)} %all-gather.3.cloned.1.call-done, f32[3456]{0:T(1024)S(1)} %copy-done.9), kind=kOutput, calls=%fused_computation.99 | convolution fusion | flops 907804672 | bytes 10630656 | tf_op jit(solution)/shard_map/dot_general | solution.py:162
  110.7 5.4 %fusion.66 = bf16[128,3456]{1,0:T(8,128)(2,1)S(1)} fusion(f32[128,3456]{1,0:T(8,128)} %fusion.65, bf16[3456,512]{0,1:T(8,128)(2,1)} %all-gather.3.cloned.1.call-done, bf16[512,3456]{1,0:T(8,128)(2,1)} %all-gather.5.cloned.1.call-done, bf16[128,3456]{1,0:T(8,128)(2,1)S(1)} %copy.50, bf16[128,3456]{1,0:T(8,128)(2,1)S(1)} %copy-done.8), kind=kOutput, calls=%fused_computation.100 | convolution fusion | flops 908689408 | bytes 11501568 | tf_op jit(solution)/shard_map/dot_general | solution.py:171
  116.2 1.3 copy.51
  117.5 2.1 slice.356
  119.6 1.9 copy.52
  121.6 0.5 fusion.98
  122.0 1.4 copy.53
  123.4 3.6 %all-to-all-start.1 = ((bf16[128,32,128]{2,0,1:T(8,128)(2,1)}), bf16[128,32,128]{2,0,1:T(8,128)(2,1)S(1)}, u32[]{:S(2)}, u32[]{:S(2)}) async-start(bf16[128,32,128]{2,0,1:T(8,128)(2,1)} %copy.53), calls=%async_computation.1 | async-start | bytes 2097152 | tf_op jit(solution)/shard_map/all_to_all | solution.py:178
  127.0 0.9 convert_reduce_fusion.2
  127.9 1.1 convert_reduce_fusion.1
  129.0 1.8 fusion.122
  130.8 1.1 fusion.123
  131.9 0.3 reduce-scatter.2.cloned.1.call-start
  132.2 10.1 %all-to-all-done.1 = bf16[128,32,128]{2,0,1:T(8,128)(2,1)S(1)} async-done(((bf16[128,32,128]{2,0,1:T(8,128)(2,1)}), bf16[128,32,128]{2,0,1:T(8,128)(2,1)S(1)}, u32[]{:S(2)}, u32[]{:S(2)}) %all-to-all-start.1) | async-done | bytes 1048608 | tf_op jit(solution)/shard_map/all_to_all | solution.py:178
  142.4 3.6 %convolution_bitcast_fusion.3 = f32[1,2048,128]{2,1,0:T(8,128)S(1)} fusion(bf16[1024,2048]{1,0:T(8,128)(2,1)} %copy-done.5, bf16[1024,4,128]{2,0,1:T(8,128)(2,1)S(1)} %bitcast.130), kind=kOutput, calls=%fused_computation.133 | convolution fusion | flops 536870912 | bytes 5505024 | tf_op jit(solution)/shard_map/while/body/eval_jaxpr/dot_general | solution.py:52
  146.1 1.3 convolution_bitcast_fusion.2
  147.4 0.9 copy-done.2
  148.2 1.3 convolution_bitcast_fusion.1
  149.5 0.9 copy-done.7
  150.4 1.3 convolution_bitcast_fusion
  151.8 2.2 pad_maximum_fusion
  154.6 40.6 %all-reduce = (f32[13,512]{1,0:T(8,128)}, f32[512]{0:T(512)}, f32[256]{0:T(256)}, f32[128]{0:T(128)}, f32[3456]{0:T(1024)}) all-reduce(f32[13,512]{1,0:T(8,128)S(1)} %convolution_bitcast_fusion.4, f32[512]{0:T(512)S(1)} %get-tuple-element.214, f32[256]{0:T(256)S(1)} %get-tuple-element.216, ...), channel_id=1, replica_groups=mesh['dp'=4,'table'=8] {'dp','table'}, use_global_device_ids=true, to_apply=%region_1.2 | all-reduce | flops 11008 | bytes 88064 | tf_op jit(solution)/shard_map/psum | solution.py:194
  195.2 69.1 %all-reduce.4.cloned.1.call-done = (f32[512,256]{1,0:T(8,128)}, f32[256,128]{1,0:T(8,128)}) async-done(((f32[512,256]{1,0:T(8,128)}, f32[256,128]{1,0:T(8,128)}), (f32[512,256]{1,0:T(8,128)}, f32[256,128]{1,0:T(8,128)})) %all-reduce.4.cloned.1.call-update) | async-done | bytes 655376 | tf_op jit(solution)/shard_map/psum | solution.py:194
  264.3 78.6 %reduce-scatter.2.cloned.1.call-done = f32[4,512,128]{2,1,0:T(8,128)} async-done(((f32[4,2048,128]{2,1,0:T(8,128)}), f32[4,512,128]{2,1,0:T(8,128)}) %reduce-scatter.2.cloned.1.call-update) | async-done | bytes 1048592 | tf_op jit(solution)/shard_map/reduce_scatter | solution.py:192
  342.9 1.9 copy.59
  344.8 1.6 copy.60
  (52 shorter events, 1.9 us)
Async XLA Ops:
  7.2 76.3 %copy-start = (bf16[512,256]{1,0:T(8,128)(2,1)S(1)}, bf16[512,256]{1,0:T(8,128)(2,1)}, u32[]{:S(2)}) copy-start(bf16[512,256]{1,0:T(8,128)(2,1)} %param.22) | copy-start | bytes 786436
  7.2 19.8 %copy-start.14 = (bf16[4,2048,128]{2,1,0:T(8,128)(2,1)S(1)}, bf16[4,2048,128]{2,1,0:T(8,128)(2,1)}, u32[]{:S(2)}) copy-start(bf16[4,2048,128]{2,1,0:T(8,128)(2,1)} %param.19) | copy-start | bytes 6291460
  7.2 97.2 %all-gather.3.cloned.1.call-start = ((), (), s32[]{:S(2)}) async-start(), calls=%async_computation.3 | async-start | bytes 3981312 | tf_op jit(solution)/shard_map/all_gather | solution.py:157
  7.9 96.5 %all-gather.5.cloned.1.call-start = ((), (), s32[]{:S(2)}) async-start(), calls=%async_computation.4 | async-start | bytes 3981312 | tf_op jit(solution)/shard_map/all_gather | solution.py:158
  27.0 15.8 %copy-start.1 = (bf16[1024,2048]{1,0:T(8,128)(2,1)}, bf16[1024,2048]{1,0:T(8,128)(2,1)S(1)}, u32[]{:S(2)}) copy-start(bf16[1024,2048]{1,0:T(8,128)(2,1)S(1)} %fusion.74) | copy-start | bytes 12582916
  42.8 15.7 %copy-start.3 = (bf16[1024,2048]{1,0:T(8,128)(2,1)}, bf16[1024,2048]{1,0:T(8,128)(2,1)S(1)}, u32[]{:S(2)}) copy-start(bf16[1024,2048]{1,0:T(8,128)(2,1)S(1)} %fusion.81) | copy-start | bytes 12582916
  58.5 15.7 %copy-start.5 = (bf16[1024,2048]{1,0:T(8,128)(2,1)}, bf16[1024,2048]{1,0:T(8,128)(2,1)S(1)}, u32[]{:S(2)}) copy-start(bf16[1024,2048]{1,0:T(8,128)(2,1)S(1)} %fusion.88) | copy-start | bytes 12582916
  74.3 2.0 copy-start.6
  75.6 7.7 %copy-start.10 = (bf16[13,512]{1,0:T(8,128)(2,1)S(1)}, bf16[13,512]{1,0:T(8,128)(2,1)}, u32[]{:S(2)}) copy-start(bf16[13,512]{1,0:T(8,128)(2,1)} %param.20) | copy-start | bytes 39940
  75.6 7.7 %copy-start.11 = (bf16[128,13]{0,1:T(8,128)(2,1)S(1)}, bf16[128,13]{0,1:T(8,128)(2,1)}, u32[]{:S(2)}) copy-start(bf16[128,13]{0,1:T(8,128)(2,1)} %param.15) | copy-start | bytes 9988
  75.6 7.7 %copy-start.12 = (f32[512]{0:T(512)S(1)}, f32[512]{0:T(512)}, u32[]{:S(2)}) copy-start(f32[512]{0:T(512)} %param.21) | copy-start | bytes 6148
  75.6 7.9 %copy-start.16 = (f32[256]{0:T(256)S(1)}, f32[256]{0:T(256)}, u32[]{:S(2)}) copy-start(f32[256]{0:T(256)} %param.23) | copy-start | bytes 3076
  75.6 8.1 %copy-start.15 = (bf16[256,128]{1,0:T(8,128)(2,1)S(1)}, bf16[256,128]{1,0:T(8,128)(2,1)}, u32[]{:S(2)}) copy-start(bf16[256,128]{1,0:T(8,128)(2,1)} %param.24) | copy-start | bytes 196612
  75.6 8.1 %copy-start.17 = (f32[128]{0:T(128)S(1)}, f32[128]{0:T(128)}, u32[]{:S(2)}) copy-start(f32[128]{0:T(128)} %param.25) | copy-start | bytes 1540
  76.3 22.8 %copy-start.13 = (s32[32]{0:T(128)S(1)}, s32[32]{0:T(128)}, u32[]{:S(2)}) copy-start(s32[32]{0:T(128)} %param.18) | copy-start | bytes 388
  78.1 20.6 %all-to-all-start = ((bf16[1024,4,128]{2,1,0:T(4,128)(2,1)}), bf16[1024,4,128]{2,1,0:T(4,128)(2,1)S(1)}, u32[]{:S(2)}, u32[]{:S(2)}) async-start(bf16[1024,4,128]{2,1,0:T(4,128)(2,1)} %copy.45), calls=%async_computation | async-start | bytes 2097152 | tf_op jit(solution)/shard_map/all_to_all | solution.py:138
  83.7 14.9 %copy-start.18 = (f32[128,256]{1,0:T(8,128)}, f32[128,256]{1,0:T(8,128)S(1)}, u32[]{:S(2)}) copy-start(f32[128,256]{1,0:T(8,128)S(1)} %convolution_add_fusion.3) | copy-start | bytes 393220
  99.0 5.4 %copy-start.8 = (bf16[128,3456]{1,0:T(8,128)(2,1)S(1)}, bf16[128,3456]{1,0:T(8,128)(2,1)}, u32[]{:S(2)}) copy-start(bf16[128,3456]{1,0:T(8,128)(2,1)} %param.29) | copy-start | bytes 2654212
  99.0 5.4 %copy-start.9 = (f32[3456]{0:T(1024)S(1)}, f32[3456]{0:T(1024)}, u32[]{:S(2)}) copy-start(f32[3456]{0:T(1024)} %param.28) | copy-start | bytes 41476
  123.4 18.9 %all-to-all-start.1 = ((bf16[128,32,128]{2,0,1:T(8,128)(2,1)}), bf16[128,32,128]{2,0,1:T(8,128)(2,1)S(1)}, u32[]{:S(2)}, u32[]{:S(2)}) async-start(bf16[128,32,128]{2,0,1:T(8,128)(2,1)} %copy.53), calls=%async_computation.1 | async-start | bytes 2097152 | tf_op jit(solution)/shard_map/all_to_all | solution.py:178
  127.0 137.3 %all-reduce.4.cloned.1.call-start = ((), (), s32[]{:S(2)}) async-start(), calls=%async_computation.6 | async-start | bytes 1310720 | tf_op jit(solution)/shard_map/psum | solution.py:194
  131.9 211.0 %reduce-scatter.2.cloned.1.call-start = ((), (), s32[]{:S(2)}) async-start(), calls=%async_computation.5 | async-start | bytes 5242880 | tf_op jit(solution)/shard_map/reduce_scatter | solution.py:192
  142.3 3.7 %copy-start.4 = (bf16[1024,2048]{1,0:T(8,128)(2,1)S(1)}, bf16[1024,2048]{1,0:T(8,128)(2,1)}, u32[]{:S(2)}) copy-start(bf16[1024,2048]{1,0:T(8,128)(2,1)} %copy-done.3) | copy-start | bytes 12582916
  146.0 2.2 copy-start.2
  148.2 2.2 copy-start.7
Sparse Core Ops, SparseCore 0:
  9.9 36.6 all-gather.2
  48.5 33.9 all-gather.4
  133.6 130.6 all-reduce.3
  267.1 75.7 reduce-scatter.1
where the time goes:
time: 354 us; the launch traced here: 353 us
  waiting for transfers between devices  174 us (49%)
  other arithmetic  64.2 us (18%)
  blocking collectives  40.6 us (11%)
  matrix products  30.2 us (9%)
  local copies, waits for them, and re-layouts  20.8 us (6%)
  between operations  14.2 us (4%)
  starting transfers between devices  9.11 us (3%)
    reduce_scatter x1, waiting for transfers between devices, local(): lax.psum_scatter(local_grad, 'dp', scatter_dimension=1, tiled=True)  78.6 us
    psum x1, waiting for transfers between devices, local(): lax.psum((partial_grads[0], partial_grads[1], partial_grads[2], partial_g...  69.1 us
    add x4, other arithmetic, hit_counts(): totals = totals + matched.astype(jnp.bfloat16)  57.9 us
    psum x1, blocking collectives, local(): lax.psum((partial_grads[0], partial_grads[1], partial_grads[2], partial_g...  40.6 us
    all_to_all x1, waiting for transfers between devices, local(): lax.all_to_all(pooled, 'table', split_axis=0, concat_axis=1, tiled=True)  14.5 us
    all_to_all x1, waiting for transfers between devices, local(): lax.all_to_all(shard_grads, 'table', split_axis=1, concat_axis=0, tiled=T...  10.1 us
    dot_general x4, matrix products, shard_one_block(): lax.dot_general(hit_table, inputs[2], (((0,), (0,)), ((), ())), preferred...  7.53 us
  transfers between devices with their start and end apart: 6, of which 4 were waited for; matrix products, arithmetic and copies ran while one was open for 26% of the time, Pallas kernels for 0%

commit v1 on v0

v1 whole, which is shorter than its diff:
```python
import functools

import jax
import jax.numpy as jnp
from jax import lax
from jax.experimental import pallas as pl
from jax.experimental.pallas import tpu as pltpu
from jax.sharding import PartitionSpec as P

TABLES = 26
MESH = pl.DeviceIdType.MESH
BF16 = jnp.bfloat16
F32 = jnp.float32
ROW_TILE = 16
CONTRACT = (((0,), (0,)), ((), ()))
BACK_DIMS = (((1,), (1,)), ((), ()))


def silu_slope(value):
    sigmoid = 1.0 / (1.0 + jnp.exp(-value))
    return sigmoid * (1.0 + value * (1.0 - sigmoid))


def row_code(index):
    low = lax.bitwise_and(index, 127) + 128
    return (low.astype(F32) * lax.shift_left(1, lax.shift_right_logical(index, 7)).astype(F32)).astype(BF16)


def remote(src, dst, send, recv, axis, peer):
    return pltpu.make_async_remote_copy(
        src_ref=src, dst_ref=dst, send_sem=send, recv_sem=recv,
        device_id={axis: peer}, device_id_type=MESH,
    )


def forward_kernel(
    n_table, codes_ref, rowcode_ref, tables_ref, down_ref, up_ref,
    hits_ref, arrived_ref, down_all, up_all,
    hit_buf, table_t, pooled_buf, hit_sem, self_sem, own_sem,
    send_sem, recv_sem, w_send, w_recv, f_send, f_recv,
):
    local_shards, slots, _, batch = codes_ref.shape
    rows = tables_ref.shape[1]
    width = tables_ref.shape[2]
    examples = batch // n_table
    chips = n_table // 2
    lanes = 2 * examples
    me = lax.axis_index("table")
    chip = me // 2
    core = lax.rem(me, 2)
    sibling = chip * 2 + 1 - core

    barrier = pltpu.get_barrier_semaphore()
    for step in range(1, n_table):
        pl.semaphore_signal(
            barrier, inc=1, device_id={"table": lax.rem(me + step, n_table)}, device_id_type=MESH
        )
    own = [
        pltpu.make_async_copy(down_ref, down_all.at[me], own_sem.at[0]),
        pltpu.make_async_copy(up_ref, up_all.at[me], own_sem.at[1]),
    ]
    for copy in own:
        copy.start()
    pl.semaphore_wait(barrier, n_table - 1)

    weights = ((down_ref, down_all), (up_ref, up_all))
    first_stage = []
    for kind, (src, dst) in enumerate(weights):
        for step in range(1, chips):
            peer = lax.rem(chip + step, chips) * 2 + core
            first_stage.append((kind, step, remote(
                src, dst.at[me], w_send.at[kind, step], w_recv.at[kind, step], "table", peer)))
        first_stage.append((kind, 0, remote(
            src, dst.at[me], w_send.at[kind, 0], w_recv.at[kind, 0], "table", sibling)))
    for _, _, copy in first_stage:
        copy.start()

    def send_to(shard, step, other):
        target = lax.rem(chip + step, chips) * 2 + other
        block = pooled_buf.at[shard, step, other]
        return remote(
            block, arrived_ref.at[me, shard], send_sem.at[shard, step, other],
            recv_sem.at[shard, step, core], "table", target)

    def recv_from(shard, step, other):
        source = lax.rem(chip + chips - step, chips) * 2 + other
        return remote(
            pooled_buf.at[shard, step, other], arrived_ref.at[source, shard],
            send_sem.at[shard, step, other], recv_sem.at[shard, step, other], "table", sibling)

    one = jnp.ones((ROW_TILE, lanes), BF16)
    zero = jnp.zeros((ROW_TILE, lanes), BF16)
    for shard in range(local_shards):
        slot = shard % 2
        if shard >= 2:
            pltpu.make_async_copy(hit_buf.at[slot], hits_ref.at[shard - 2], hit_sem.at[shard - 2]).wait()
        table_t[...] = tables_ref[shard].T

        def one_chunk(step):
            target_chip = lax.rem(chip + step, chips)
            start = pl.multiple_of(target_chip * lanes, lanes)
            codes = [codes_ref[shard, h, :, pl.ds(start, lanes)] for h in range(slots)]

            @pl.loop(0, rows // ROW_TILE, unroll=4)
            def _(tile):
                begin = pl.multiple_of(tile * ROW_TILE, ROW_TILE)
                code = rowcode_ref[pl.ds(begin, ROW_TILE), :]
                code = jnp.concatenate([code] * (lanes // 128), axis=1)
                found = [jnp.where(item == code, one, zero) for item in codes]
                while len(found) > 1:
                    found = [found[i] + found[i + 1] for i in range(0, len(found) - 1, 2)] + (
                        [found[-1]] if len(found) % 2 else [])
                hit_buf[slot, pl.ds(begin, ROW_TILE), pl.ds(start, lanes)] = found[0]

            pooled = jnp.dot(
                table_t[...], hit_buf[slot, :, pl.ds(start, lanes)], preferred_element_type=F32)
            pooled = pooled.T.astype(BF16)
            for other in range(2):
                pooled_buf[shard, step, other] = pooled[other * examples:(other + 1) * examples]

        @pl.loop(1, chips)
        def _(step):
            one_chunk(step)
            for other in range(2):
                send_to(shard, step, other).start()

        one_chunk(0)
        send_to(shard, 0, 1 - core).start()
        pltpu.make_async_copy(
            pooled_buf.at[shard, 0, core], arrived_ref.at[me, shard], self_sem.at[shard]).start()
        pltpu.make_async_copy(hit_buf.at[slot], hits_ref.at[shard], hit_sem.at[shard]).start()

    second_stage = []
    for kind, step, copy in first_stage:
        copy.wait_recv()
        if step:
            src = lax.rem(chip + chips - step, chips) * 2 + core
            whole = weights[kind][1]
            forward = remote(
                whole.at[src], whole.at[src], f_send.at[kind, step], f_recv.at[kind, step],
                "table", sibling)
            forward.start()
            second_stage.append(forward)
    for shard in range(local_shards):
        send_to(shard, 0, 1 - core).wait_send()
        recv_from(shard, 0, 1 - core).wait_recv()
        pltpu.make_async_copy(
            pooled_buf.at[shard, 0, core], arrived_ref.at[me, shard], self_sem.at[shard]).wait()
        for step in range(1, chips):
            for other in range(2):
                send_to(shard, step, other).wait_send()
                recv_from(shard, step, other).wait_recv()
    for copy in own:
        copy.wait()
    for _, _, copy in first_stage:
        copy.wait_send()
    for copy in second_stage:
        copy.wait()
    for shard in range(max(0, local_shards - 2), local_shards):
        pltpu.make_async_copy(hit_buf.at[shard % 2], hits_ref.at[shard], hit_sem.at[shard]).wait()


def forward_exchange(n_table, codes, rowcode, tables, down_t, up):
    local_shards, slots, _, batch = codes.shape
    _, rows, width = tables.shape
    examples = batch // n_table
    chips = n_table // 2
    vmem = pl.BlockSpec(memory_space=pltpu.VMEM)
    hbm = pl.BlockSpec(memory_space=pl.ANY)
    dma = pltpu.SemaphoreType.DMA
    return pl.pallas_call(
        functools.partial(forward_kernel, n_table),
        out_shape=(
            jax.ShapeDtypeStruct((local_shards, rows, batch), BF16),
            jax.ShapeDtypeStruct((n_table, local_shards, examples, width), BF16),
            jax.ShapeDtypeStruct((n_table,) + down_t.shape, BF16),
            jax.ShapeDtypeStruct((n_table,) + up.shape, BF16),
        ),
        in_specs=[vmem, vmem, vmem, hbm, hbm],
        out_specs=(hbm, hbm, hbm, hbm),
        scratch_shapes=[
            pltpu.VMEM((2, rows, batch), BF16),
            pltpu.VMEM((width, rows), BF16),
            pltpu.VMEM((local_shards, chips, 2, examples, width), BF16),
            dma((local_shards,)),
            dma((local_shards,)),
            dma((2,)),
            dma((local_shards, chips, 2)),
            dma((local_shards, chips, 2)),
            dma((2, chips)),
            dma((2, chips)),
            dma((2, chips)),
            dma((2, chips)),
        ],
        compiler_params=pltpu.CompilerParams(
            collective_id=0, has_side_effects=True, vmem_limit_bytes=40 * 1024 * 1024),
        name="pool_and_exchange",
    )(codes, rowcode, tables, down_t, up)


def backward_kernel(
    n_table, n_dp, grads_ref, hits_ref, dense_ref, first_pre, first_act, second_pre, second_act,
    third_pre, bottom_grad, second_layer, third_layer, bias_ref,
    table_out, first_out, first_bias, second_out, second_bias, third_out, third_bias, cross_bias,
    hit_buf, got, tab_send, tab_recv, part, edge, part_recv, dp_send, dp_recv, whole,
    hit_sem, a_send, a_recv, t_send, t_recv, p_send, p_recv, d_send, d_recv, w_send, w_recv,
):
    local_shards, rows, batch = hits_ref.shape
    width = grads_ref.shape[3]
    examples = batch // n_table
    chunk = rows // n_dp
    me = lax.axis_index("table")
    level = lax.axis_index("dp")
    share = part_recv.shape[1]

    hit_copies = [
        pltpu.make_async_copy(hits_ref.at[shard], hit_buf.at[shard], hit_sem.at[shard])
        for shard in range(local_shards)
    ]
    for copy in hit_copies:
        copy.start()
    barrier = pltpu.get_barrier_semaphore()
    for step in range(1, n_table):
        pl.semaphore_signal(
            barrier, inc=1, device_id={"table": lax.rem(me + step, n_table)}, device_id_type=MESH)
    for step in range(1, n_dp):
        pl.semaphore_signal(
            barrier, inc=1, device_id={"dp": lax.rem(level + step, n_dp)}, device_id_type=MESH)
    pl.semaphore_wait(barrier, n_table + n_dp - 2)

    def grad_copy(shard, step):
        peer = lax.rem(me + step, n_table)
        return remote(
            grads_ref.at[peer, shard], got.at[shard, me], a_send.at[shard, step],
            a_recv.at[shard, step], "table", peer)

    for shard in range(local_shards):
        for step in range(1, n_table):
            grad_copy(shard, step).start()
        got[shard, me] = grads_ref[me, shard]

    def table_copy(shard, step):
        return remote(
            tab_send.at[shard, step - 1], tab_recv.at[shard, step - 1], t_send.at[shard, step],
            t_recv.at[shard, step], "dp", lax.rem(level + step, n_dp))

    def shard_step(shard):
        for step in range(1, n_table):
            grad_copy(shard, step).wait_recv()
        hit_copies[shard].wait()
        rows_grad = got[shard].reshape(batch, width)

        def product(step):
            begin = pl.multiple_of(lax.rem(level + step, n_dp) * chunk, chunk)
            return jnp.dot(
                hit_buf[shard, pl.ds(begin, chunk), :], rows_grad, preferred_element_type=F32)

        for step in range(1, n_dp):
            tab_send[shard, step - 1] = product(step).astype(BF16)
            table_copy(shard, step).start()
        table_out[shard] = product(0)

    def part_copy(step):
        peer = lax.rem(me + step, n_table)
        return remote(
            part.at[pl.ds(pl.multiple_of(peer * share, 16), share)], part_recv.at[step - 1],
            p_send.at[step], p_recv.at[step], "table", peer)

    def dp_copy(step):
        return remote(
            dp_send, dp_recv.at[step - 1], d_send.at[step], d_recv.at[step], "dp",
            lax.rem(level + step, n_dp))

    def whole_block(index):
        return whole.at[pl.ds(pl.multiple_of(index * share, 16), share)]

    def whole_copy(step):
        return remote(
            whole_block(me), whole_block(me), w_send.at[step], w_recv.at[step], "table",
            lax.rem(me + step, n_table))

    first_width = first_pre.shape[1]
    second_width = second_pre.shape[1]
    pad_in = dense_ref.shape[1]
    first_tiles = first_width // 128
    second_tiles = second_width // 128
    third_base = second_tiles * first_width
    dense_base = third_base + second_width
    edge_base = dense_base + first_tiles * pad_in
    edge_rows = edge.shape[0]

    def bottom_back():
        edge[...] = jnp.zeros_like(edge)
        third_delta = (
            silu_slope(third_pre[...]) * bottom_grad[...].astype(F32)).astype(BF16)
        third_grad = lax.dot_general(
            second_act[...], third_delta, CONTRACT, preferred_element_type=F32)
        part[third_base:third_base + second_width, :] = third_grad.astype(BF16)
        second_back = lax.dot_general(
            third_delta, third_layer[...], BACK_DIMS, preferred_element_type=F32)
        second_delta = (silu_slope(second_pre[...]) * second_back).astype(BF16)
        second_grad = lax.dot_general(
            first_act[...], second_delta, CONTRACT, preferred_element_type=F32).astype(BF16)
        for tile in range(second_tiles):
            part[tile * first_width:(tile + 1) * first_width, :] = second_grad[
                :, tile * 128:(tile + 1) * 128]
        first_back = lax.dot_general(
            second_delta, second_layer[...], BACK_DIMS, preferred_element_type=F32)
        first_delta = (silu_slope(first_pre[...]) * first_back).astype(BF16)
        first_grad = lax.dot_general(
            dense_ref[...], first_delta, CONTRACT, preferred_element_type=F32).astype(BF16)
        for tile in range(first_tiles):
            part[dense_base + tile * pad_in:dense_base + (tile + 1) * pad_in, :] = first_grad[
                :, tile * 128:(tile + 1) * 128]
        row = 0
        for delta, tiles in (
            (first_delta, first_tiles), (second_delta, second_tiles), (third_delta, 1)
        ):
            total = jnp.sum(delta.astype(F32), axis=0, keepdims=True)
            for tile in range(tiles):
                edge[row:row + 1, :] = total[:, tile * 128:(tile + 1) * 128]
                row += 1
        edge[8:8 + bias_ref.shape[0], :] = bias_ref[...]
        part[edge_base:edge_base + edge_rows, :] = edge[...].astype(BF16)
        left = part.shape[0] - edge_base - edge_rows
        if left:
            part[edge_base + edge_rows:, :] = jnp.zeros((left, 128), BF16)

    shard_step(0)
    bottom_back()
    for step in range(1, n_table):
        part_copy(step).start()
    for shard in range(1, local_shards):
        shard_step(shard)

    total = part[pl.ds(pl.multiple_of(me * share, 16), share), :].astype(F32)
    for step in range(1, n_table):
        part_copy(step).wait_recv()
        total = total + part_recv[step - 1].astype(F32)
    dp_send[...] = total.astype(BF16)
    for step in range(1, n_dp):
        dp_copy(step).start()
    for step in range(1, n_dp):
        dp_copy(step).wait_recv()
        total = total + dp_recv[step - 1].astype(F32)
    whole[pl.ds(pl.multiple_of(me * share, 16), share), :] = total.astype(BF16)
    for step in range(1, n_table):
        whole_copy(step).start()

    for shard in range(local_shards):
        for step in range(1, n_dp):
            table_copy(shard, step).wait_recv()
            table_out[shard] += tab_recv[shard, step - 1].astype(F32)
    for step in range(1, n_table):
        whole_copy(step).wait_recv()
    for tile in range(second_tiles):
        second_out[:, tile * 128:(tile + 1) * 128] = whole[
            tile * first_width:(tile + 1) * first_width, :].astype(F32)
    third_out[...] = whole[third_base:third_base + second_width, :].astype(F32)
    for tile in range(first_tiles):
        block = whole[dense_base + tile * pad_in:dense_base + (tile + 1) * pad_in, :].astype(F32)
        first_out[:, tile * 128:(tile + 1) * 128] = block[:first_out.shape[0]]
    edge[...] = whole[edge_base:edge_base + edge_rows, :].astype(F32)
    first_bias[...] = edge[0:first_tiles, :]
    second_bias[...] = edge[first_tiles:first_tiles + second_tiles, :]
    third_bias[...] = edge[first_tiles + second_tiles:first_tiles + second_tiles + 1, :]
    cross_bias[...] = edge[8:8 + cross_bias.shape[0], :]

    for shard in range(local_shards):
        for step in range(1, n_table):
            grad_copy(shard, step).wait_send()
        for step in range(1, n_dp):
            table_copy(shard, step).wait_send()
    for step in range(1, n_table):
        part_copy(step).wait_send()
        whole_copy(step).wait_send()
    for step in range(1, n_dp):
        dp_copy(step).wait_send()


def backward_exchange(n_table, n_dp, grads, hits, dense, first_pre, first_act, second_pre,
                      second_act, third_pre, bottom_grad, second_layer, third_layer, bias_part,
                      dense_width):
    local_shards, rows, batch = hits.shape
    width = grads.shape[3]
    first_width = first_pre.shape[1]
    second_width = second_pre.shape[1]
    bias_rows = bias_part.shape[0]
    edge_rows = -(-(8 + bias_rows) // 16) * 16
    used = (second_width // 128 * first_width + second_width
            + first_width // 128 * dense.shape[1] + edge_rows)
    share = -(-used // (16 * n_table)) * 16
    vmem = pl.BlockSpec(memory_space=pltpu.VMEM)
    hbm = pl.BlockSpec(memory_space=pl.ANY)
    dma = pltpu.SemaphoreType.DMA
    shapes = (
        (local_shards, rows // n_dp, width), (dense_width, first_width), (first_width // 128, 128),
        (first_width, second_width), (second_width // 128, 128), (second_width, width), (1, 128),
        (bias_rows, 128),
    )
    return pl.pallas_call(
        functools.partial(backward_kernel, n_table, n_dp),
        out_shape=tuple(jax.ShapeDtypeStruct(shape, F32) for shape in shapes),
        in_specs=[vmem, hbm] + [vmem] * 10,
        out_specs=(vmem,) * 8,
        scratch_shapes=[
            pltpu.VMEM((local_shards, rows, batch), BF16),
            pltpu.VMEM((local_shards, n_table, batch // n_table, width), BF16),
            pltpu.VMEM((local_shards, n_dp - 1, rows // n_dp, width), BF16),
            pltpu.VMEM((local_shards, n_dp - 1, rows // n_dp, width), BF16),
            pltpu.VMEM((n_table * share, 128), BF16),
            pltpu.VMEM((edge_rows, 128), F32),
            pltpu.VMEM((n_table - 1, share, 128), BF16),
            pltpu.VMEM((share, 128), BF16),
            pltpu.VMEM((n_dp - 1, share, 128), BF16),
            pltpu.VMEM((n_table * share, 128), BF16),
            dma((local_shards,)),
            dma((local_shards, n_table)),
            dma((local_shards, n_table)),
            dma((local_shards, n_dp)),
            dma((local_shards, n_dp)),
            dma((n_table,)),
            dma((n_table,)),
            dma((n_dp,)),
            dma((n_dp,)),
            dma((n_table,)),
            dma((n_table,)),
        ],
        compiler_params=pltpu.CompilerParams(
            collective_id=1, has_side_effects=True, vmem_limit_bytes=48 * 1024 * 1024),
        name="gradient_exchange",
    )(grads, hits, dense, first_pre, first_act, second_pre, second_act, third_pre, bottom_grad,
      second_layer, third_layer, bias_part)


def bottom_pass(
    dense_rows, first_layer, first_offset, second_layer, second_offset, third_layer, third_offset
):
    first_pre = jnp.dot(dense_rows, first_layer, preferred_element_type=F32) + first_offset
    first_act = jax.nn.silu(first_pre).astype(BF16)
    second_pre = jnp.dot(first_act, second_layer, preferred_element_type=F32) + second_offset
    second_act = jax.nn.silu(second_pre).astype(BF16)
    third_pre = jnp.dot(second_act, third_layer, preferred_element_type=F32) + third_offset
    bottom_out = jax.nn.silu(third_pre).astype(BF16)
    return (bottom_out, (first_pre, first_act, second_pre, second_act, third_pre))


def local(
    n_table,
    n_dp,
    dense_feats,
    lookup_ids,
    lookup_counts,
    shard_table,
    embed_tables,
    first_layer,
    first_offset,
    second_layer,
    second_offset,
    third_layer,
    third_offset,
    cross_down,
    cross_up,
    cross_bias,
    cotangent,
):
    local_shards, rows, width = embed_tables.shape
    slots, batch = lookup_ids.shape[1:]
    examples, dense_width = dense_feats.shape
    shard_total = local_shards * n_table

    slot_iota = lax.broadcasted_iota(jnp.int32, (1, slots, 1), 1)
    codes = jnp.where(lookup_counts[:, None, :] > slot_iota, row_code(lookup_ids), 0).astype(BF16)
    codes = jnp.broadcast_to(codes[:, :, None, :], (local_shards, slots, ROW_TILE, batch))
    rowcode = row_code(lax.broadcasted_iota(jnp.int32, (rows, 128), 0))
    hits, arrived, down_all, up_all = forward_exchange(
        n_table, codes, rowcode, embed_tables, cross_down.T, cross_up)
    down_t = down_all.reshape(-1, cross_up.shape[1])
    up_whole = up_all.reshape(-1, cross_up.shape[1])

    table_onehot = (
        shard_table[:, None] == lax.broadcasted_iota(jnp.int32, (shard_total, TABLES), 1)
    ).astype(BF16)
    table_pooled = jnp.einsum(
        "sbe,st->bte", arrived.reshape(shard_total, examples, width), table_onehot,
        preferred_element_type=F32).astype(BF16)
    bottom_out, saved = bottom_pass(
        dense_feats, first_layer, first_offset, second_layer, second_offset, third_layer,
        third_offset)
    cross_input = jnp.concatenate([bottom_out[:, None, :], table_pooled], axis=1).reshape(
        examples, -1)
    low_rank = lax.dot_general(
        cross_input, down_t, BACK_DIMS, preferred_element_type=F32).astype(BF16)
    mixing = jnp.dot(low_rank, up_whole, preferred_element_type=F32) + cross_bias
    cot_float = cotangent.astype(F32)
    mix_grad = cot_float * cross_input.astype(F32)
    bias_part = jnp.sum(mix_grad, axis=0)
    rank_grad = lax.dot_general(
        mix_grad.astype(BF16), up_whole, BACK_DIMS, preferred_element_type=F32).astype(BF16)
    input_grad = (
        cot_float * (mixing + 1.0) + jnp.dot(rank_grad, down_t, preferred_element_type=F32)
    ).astype(BF16)
    bottom_grad = input_grad[:, :width]
    shard_grads = jnp.einsum(
        "bte,st->sbe", input_grad.reshape(examples, TABLES + 1, width)[:, 1:, :], table_onehot,
        preferred_element_type=F32).astype(BF16)
    dense_pad = jnp.pad(dense_feats, ((0, 0), (0, -dense_width % 16)))
    outs = backward_exchange(
        n_table, n_dp, shard_grads.reshape(n_table, local_shards, examples, width), hits,
        dense_pad, *saved, bottom_grad, second_layer, third_layer, bias_part.reshape(-1, 128),
        dense_width)
    return (outs[0], outs[1], outs[2].reshape(-1), outs[3], outs[4].reshape(-1), outs[5],
            outs[6].reshape(-1), outs[7].reshape(-1))


def solution(mesh):
    placed = (
        P(("dp", "table"), None),
        P("table", None, "dp"),
        P("table", "dp"),
        P(),
        P("table", None, None),
        P(),
        P(),
        P(),
        P(),
        P(),
        P(),
        P(None, "table"),
        P("table", None),
        P(),
        P(("dp", "table"), None),
    )
    return jax.shard_map(
        functools.partial(local, mesh.shape["table"], mesh.shape["dp"]),
        mesh=mesh,
        in_specs=placed,
        out_specs=(P("table", "dp", None), P(), P(), P(), P(), P(), P(), P()),
        check_vma=False,
    )
```

time: 354 us -> 161 us (0.45)
  waiting for transfers between devices: 174 us -> 0 us
  Pallas kernels: 0 us -> 122 us
  other arithmetic: 64.2 us -> 1.81 us
  blocking collectives: 40.6 us -> 0 us
  between operations: 14.2 us -> 1.04 us
  matrix products: 30.2 us -> 17.4 us
  starting transfers between devices: 9.11 us -> 0 us
    pallas_call x0 -> x2, Pallas kernels: none -> 122 us  [the longest x1 67.1 us: backward_exchange(): pl.pallas_call(functools.partial(backward_kernel, n_table, n_dp), out_sha...]
    reduce_scatter x1 -> x0, waiting for transfers between devices: 78.6 us -> none  [local(): lax.psum_scatter(local_grad, 'dp', scatter_dimension=1, tiled=True)]
    psum x1 -> x0, waiting for transfers between devices: 69.1 us -> none  [local(): lax.psum((partial_grads[0], partial_grads[1], partial_grads[2], partial_g...]
    add x4 -> x0, other arithmetic: 57.9 us -> none  [hit_counts(): totals = totals + matched.astype(jnp.bfloat16)]
    psum x1 -> x0, blocking collectives: 40.6 us -> none  [local(): lax.psum((partial_grads[0], partial_grads[1], partial_grads[2], partial_g...]
    all_to_all x2 -> x0, waiting for transfers between devices: 24.6 us -> none  [the longest x1 14.5 us: local(): lax.all_to_all(pooled, 'table', split_axis=0, concat_axis=1, tiled=True)]
    dot_general x20 -> x7, matrix products: 30.2 us -> 17.4 us  [the longest x1 5.9 us: local(): jnp.dot(rank_grad, down_t, preferred_element_type=F32)]
    all_to_all x2 -> x0, starting transfers between devices: 8.73 us -> none  [the longest x1 5.17 us: local(): lax.all_to_all(pooled, 'table', split_axis=0, concat_axis=1, tiled=True)]
  transfers between devices with their start and end apart: 6 -> 0, of which waited for: 4 -> 0; matrix products, arithmetic and copies ran while one was open for 26% -> 0% of each run, Pallas kernels for 0% -> 0%
where the time goes in v1:
time: 161 us
  Pallas kernels  122 us (76%)
  local copies, waits for them, and re-layouts  18.3 us (11%)
  matrix products  17.4 us (11%)
  other arithmetic  1.81 us (1%)
    pallas_call x1, Pallas kernels, backward_exchange(): pl.pallas_call(functools.partial(backward_kernel, n_table, n_dp), out_sha...  67.1 us
    pallas_call x1, Pallas kernels, forward_exchange(): pl.pallas_call(functools.partial(forward_kernel, n_table), out_shape=(jax...  55.4 us
    unnamed x56, local copies, waits for them, and re-layouts  9.87 us
    dot_general x1, matrix products, local(): jnp.dot(rank_grad, down_t, preferred_element_type=F32)  5.9 us
    dot_general x1, matrix products, local(): jnp.dot(low_rank, up_whole, preferred_element_type=F32) + cross_bias  5.59 us

profile of v1, /device:TPU:0, one launch (start us, length us, event | category | flops | bytes accessed | tf_op | source)
XLA Modules:
  0.0 161.0 jit_solution(15163369300039567196)
XLA Ops:
  0.6 0.0 copy-start
  0.7 0.0 copy-start.9
  0.7 0.0 copy-start.18
  0.7 0.0 copy-start.19
  0.7 0.0 copy-start.5
  0.7 0.0 copy-start.2
  0.7 0.6 copy-done
  1.4 1.9 %multiply_convert_fusion = (bf16[128,512]{1,0:T(8,128)(2,1)S(1)}, f32[128,512]{1,0:T(8,128)}) fusion(f32[512]{0:T(512)} %param.21, bf16[128,13]{0,1:T(8,128)(2,1)} %param.15, bf16[13,512]{1,0:T(8,128)(2,1)S(1)} %copy-done), kind=kOutput, calls=%fused_computation.18 | convolution fusion | flops 2097152 | bytes 411904 | tf_op jit(solution)/shard_map/dot_general | solution.py:439
  3.3 1.8 %multiply_convert_fusion.2 = (bf16[128,256]{1,0:T(8,128)(2,1)S(1)}, f32[128,256]{1,0:T(8,128)}) fusion(f32[256]{0:T(256)} %param.23, bf16[128,512]{1,0:T(8,128)(2,1)S(1)} %get-tuple-element.32.first_act, bf16[512,256]{1,0:T(8,128)(2,1)} %second_layer.1), kind=kOutput, calls=%fused_computation.21 | convolution fusion | flops 33751040 | bytes 590848 | tf_op jit(solution)/shard_map/dot_general | solution.py:441
  5.1 0.8 convolution_add_fusion.4.third_pre
  6.0 0.1 copy.32
  6.1 0.5 copy-done.3
  6.6 0.1 broadcast_in_dim.10.codes_ref
  6.8 0.3 iota.18.rowcode_ref
  7.1 0.0 copy-start.21
  7.1 55.4 %pool_and_exchange.1 = (bf16[4,2048,1024]{2,1,0:T(8,128)(2,1)}, bf16[8,4,128,128]{3,2,1,0:T(8,128)(2,1)S(1)}, bf16[8,64,3456]{2,1,0:T(8,128)(2,1)S(1)}, bf16[8,64,3456]{2,1,0:T(8,128)(2,1)S(1)}) custom-call(bf16[4,8,16,1024]{3,2,1,0:T(8,128)(2,1)S(1)} %broadcast_in_dim.10.codes_ref, bf16[2048,128]{1,0:T(8,128)(2,1)S(1)} %iota.18.rowcode_ref, ...), custom_call_target="tpu_custom_call" | custom-call | tf_op jit(solution)/shard_map/pool_and_exchange/pallas_call | solution.py:171
  62.5 1.8 %copy-done.1 = bf16[8,64,3456]{2,1,0:T(8,128)(2,1)} copy-done((bf16[8,64,3456]{2,1,0:T(8,128)(2,1)}, bf16[8,64,3456]{2,1,0:T(8,128)(2,1)S(1)}, u32[]{:S(2)}) %copy-start.1) | copy-done | bytes 3538968
  64.3 0.8 fusion.5
  65.1 1.5 pad_maximum_fusion
  66.6 2.6 %copy.33 = bf16[128,27,128]{0,2,1:T(8,128)(2,1)} copy(bf16[128,27,128]{2,1,0:T(8,128)(2,1)} %pad_maximum_fusion) | data formatting | bytes 1769472 | tf_op jit(solution)/shard_map/concatenate | solution.py:490
  69.2 5.6 %fusion.1 = f32[128,3456]{1,0:T(8,128)} fusion(bf16[512,3456]{1,0:T(8,128)(2,1)} %bitcast.35, bf16[128,3456]{1,0:T(8,128)(2,1)} %param.29, bf16[128,3456]{0,1:T(8,128)(2,1)} %bitcast.45, bf16[512,3456]{1,0:T(8,128)(2,1)S(1)} %bitcast.33, f32[3456]{0:T(1024)} %param.28), kind=kOutput, calls=%fused_computation.3 | convolution fusion | flops 907804672 | bytes 10630656 | tf_op jit(solution)/shard_map/dot_general | solution.py:494
  74.8 2.2 %copy.34 = bf16[128,3456]{1,0:T(8,128)(2,1)} copy(bf16[128,3456]{0,1:T(8,128)(2,1)} %bitcast.46) | data formatting | bytes 1769472 | tf_op jit(solution)/shard_map/reshape | solution.py:490
  77.0 5.9 %fusion.2 = bf16[128,3456]{1,0:T(8,128)(2,1)} fusion(f32[128,3456]{1,0:T(8,128)} %fusion.1, bf16[512,3456]{1,0:T(8,128)(2,1)S(1)} %bitcast.34, bf16[512,3456]{1,0:T(8,128)(2,1)} %bitcast.36, bf16[128,3456]{1,0:T(8,128)(2,1)} %copy.34, bf16[128,3456]{1,0:T(8,128)(2,1)} %param.29), kind=kOutput, calls=%fused_computation.4 | convolution fusion | flops 908689408 | bytes 11501568 | tf_op jit(solution)/shard_map/dot_general | solution.py:501
  82.9 1.9 %copy.35 = bf16[128,3456]{0,1:T(8,128)(2,1)S(1)} copy(bf16[128,3456]{1,0:T(8,128)(2,1)} %fusion.2) | data formatting | bytes 1769472 | tf_op jit(solution)/shard_map/convert_element_type | solution.py:502
  84.8 0.0 copy-start.22
  84.8 0.1 slice.8
  84.9 1.4 copy.42
  86.3 0.0 copy-start.16
  86.4 0.0 copy-start.17
  86.4 0.5 convolution_convert_fusion
  86.9 0.0 copy-start.20
  86.9 0.0 copy-start.7
  86.9 0.0 copy-start.8
  86.9 0.0 copy-start.10
  86.9 0.0 copy-start.15
  87.0 0.4 copy.37
  87.4 0.8 slice.9.bottom_grad
  88.1 0.3 fusion.3
  88.4 0.1 copy.38
  88.6 67.1 %gradient_exchange.1 = (f32[4,512,128]{2,1,0:T(8,128)S(1)}, f32[13,512]{1,0:T(8,128)S(1)}, f32[4,128]{1,0:T(4,128)S(1)}, f32[512,256]{1,0:T(8,128)S(1)}, f32[2,1...) custom-call(bf16[8,4,128,128]{3,2,1,0:T(8,128)(2,1)S(1)} %bitcast.37, ...), custom_call_target="tpu_custom_call" | custom-call | tf_op jit(solution)/shard_map/gradient_exchange/pallas_call | solution.py:401
  155.7 1.0 copy.53
  156.7 0.6 copy.54
  157.3 0.6 copy.55
  157.9 0.8 copy.56
  158.7 0.6 copy.57
  159.2 0.7 copy.58
  159.9 0.5 copy.59
  160.4 0.6 copy.60
  (32 shorter events, 0.2 us)
Async XLA Ops:
  0.6 0.7 copy-start
  0.7 4.5 %copy-start.9 = (bf16[256,128]{1,0:T(8,128)(2,1)S(1)}, bf16[256,128]{1,0:T(8,128)(2,1)}, u32[]{:S(2)}) copy-start(bf16[256,128]{1,0:T(8,128)(2,1)} %third_layer.1) | copy-start | bytes 196612
  0.7 5.9 %copy-start.18 = (s32[4,8,1024]{2,1,0:T(8,128)S(1)}, s32[4,8,1024]{2,1,0:T(8,128)}, u32[]{:S(2)}) copy-start(s32[4,8,1024]{2,1,0:T(8,128)} %param.16) | copy-start | bytes 393220
  0.7 5.9 %copy-start.19 = (s32[4,1024]{1,0:T(4,128)S(1)}, s32[4,1024]{1,0:T(4,128)}, u32[]{:S(2)}) copy-start(s32[4,1024]{1,0:T(4,128)} %param.17) | copy-start | bytes 49156
  0.7 6.4 %copy-start.5 = (bf16[3456,64]{0,1:T(8,128)(2,1)S(1)}, bf16[3456,64]{0,1:T(8,128)(2,1)}, u32[]{:S(2)}) copy-start(bf16[3456,64]{0,1:T(8,128)(2,1)} %param.26) | copy-start | bytes 1327108
  0.7 6.4 %copy-start.2 = (bf16[4,2048,128]{2,1,0:T(8,128)(2,1)S(1)}, bf16[4,2048,128]{2,1,0:T(8,128)(2,1)}, u32[]{:S(2)}) copy-start(bf16[4,2048,128]{2,1,0:T(8,128)(2,1)} %tables_ref.1) | copy-start | bytes 6291460
  0.7 6.4 %copy-start.6 = (bf16[64,3456]{1,0:T(8,128)(2,1)S(1)}, bf16[64,3456]{1,0:T(8,128)(2,1)}, u32[]{:S(2)}) copy-start(bf16[64,3456]{1,0:T(8,128)(2,1)} %up_ref.1) | copy-start | bytes 1327108
  3.3 2.8 %copy-start.13 = (bf16[128,512]{1,0:T(8,128)(2,1)}, bf16[128,512]{1,0:T(8,128)(2,1)S(1)}, u32[]{:S(2)}) copy-start(bf16[128,512]{1,0:T(8,128)(2,1)S(1)} %get-tuple-element.32.first_act) | copy-start | bytes 393220
  5.1 0.9 copy-start.11
  5.9 0.6 copy-start.3
  7.1 57.2 %copy-start.21 = (s32[32]{0:T(128)S(1)}, s32[32]{0:T(128)}, u32[]{:S(2)}) copy-start(s32[32]{0:T(128)} %param.18) | copy-start | bytes 388
  62.5 1.8 %copy-start.1 = (bf16[8,64,3456]{2,1,0:T(8,128)(2,1)}, bf16[8,64,3456]{2,1,0:T(8,128)(2,1)S(1)}, u32[]{:S(2)}) copy-start(bf16[8,64,3456]{2,1,0:T(8,128)(2,1)S(1)} %get-tuple-element.22) | copy-start | bytes 10616836
  84.8 1.5 copy-start.22
  86.3 1.8 %copy-start.16 = (bf16[128,3456]{1,0:T(8,128)(2,1)S(1)}, bf16[128,3456]{1,0:T(8,128)(2,1)}, u32[]{:S(2)}) copy-start(bf16[128,3456]{1,0:T(8,128)(2,1)} %copy.34) | copy-start | bytes 2654212
  86.4 1.8 %copy-start.17 = (bf16[128,3456]{1,0:T(8,128)(2,1)S(1)}, bf16[128,3456]{1,0:T(8,128)(2,1)}, u32[]{:S(2)}) copy-start(bf16[128,3456]{1,0:T(8,128)(2,1)} %param.29) | copy-start | bytes 2654212
  86.9 1.5 copy-start.20
  86.9 1.7 %copy-start.4 = (f32[128,128]{1,0:T(8,128)S(1)}, f32[128,128]{1,0:T(8,128)}, u32[]{:S(2)}) copy-start(f32[128,128]{1,0:T(8,128)} %copy-done.3) | copy-start | bytes 196612
  86.9 1.7 %copy-start.7 = (bf16[512,256]{1,0:T(8,128)(2,1)S(1)}, bf16[512,256]{1,0:T(8,128)(2,1)}, u32[]{:S(2)}) copy-start(bf16[512,256]{1,0:T(8,128)(2,1)} %second_layer.1) | copy-start | bytes 786436
  86.9 1.7 %copy-start.8 = (f32[128,512]{1,0:T(8,128)S(1)}, f32[128,512]{1,0:T(8,128)}, u32[]{:S(2)}) copy-start(f32[128,512]{1,0:T(8,128)} %get-tuple-element.33.first_pre) | copy-start | bytes 786436
  86.9 1.7 %copy-start.10 = (bf16[256,128]{1,0:T(8,128)(2,1)S(1)}, bf16[256,128]{1,0:T(8,128)(2,1)}, u32[]{:S(2)}) copy-start(bf16[256,128]{1,0:T(8,128)(2,1)} %third_layer.1) | copy-start | bytes 196612
  86.9 1.7 %copy-start.12 = (bf16[128,256]{1,0:T(8,128)(2,1)S(1)}, bf16[128,256]{1,0:T(8,128)(2,1)}, u32[]{:S(2)}) copy-start(bf16[128,256]{1,0:T(8,128)(2,1)} %copy-done.11) | copy-start | bytes 196612
  86.9 1.7 %copy-start.14 = (bf16[128,512]{1,0:T(8,128)(2,1)S(1)}, bf16[128,512]{1,0:T(8,128)(2,1)}, u32[]{:S(2)}) copy-start(bf16[128,512]{1,0:T(8,128)(2,1)} %copy-done.13) | copy-start | bytes 393220
  86.9 1.7 %copy-start.15 = (f32[128,256]{1,0:T(8,128)S(1)}, f32[128,256]{1,0:T(8,128)}, u32[]{:S(2)}) copy-start(f32[128,256]{1,0:T(8,128)} %get-tuple-element.35.second_pre) | copy-start | bytes 393220
